TPU v7x, 128 devices: a whole 4x4x4 slice. The times are simulated.
128 devices in a mesh: gx: 8 (over y, x_lo), gy: 16 (over z, x_hi, core).
Axes of the slice: x: 4 (x_hi: 2, x_lo: 2; x = x_hi * 2 + x_lo), y: 4, z: 4, core: 2. Of those that a mesh axis runs over, the one named last changes fastest.
Arguments:
- electric: float32 [3, 128, 512, 128], P(None, 'gx', 'gy'), may hold values from -6 to 6
- magnetic: float32 [3, 128, 512, 128], P(None, 'gx', 'gy'), may hold values from -6 to 6
- material_ids: int32 [128, 512, 128], P('gx', 'gy'), may hold values from 0 to 7
- material_table: float32 [8, 9], replicated, as said below
Outputs:
- electric_out: float32 [3, 128, 512, 128], P(None, 'gx', 'gy')
- magnetic_out: float32 [3, 128, 512, 128], P(None, 'gx', 'gy')
Inputs may be any that keep to these rules, and one draw needn't show every extreme that they name: `material_table`: each material's tensor is symmetric with diagonal entries above twice the sum of its off-diagonal magnitudes.
All inputs are finite; a program needn't handle non-finite values.
Results may differ from a plain program's by a relative error of at most 0.00002.
Values sent between devices are 32-bit elements; how exact they have to be, the bound alone decides.
A program may use at most 64 MiB of HBM per device.

v0:
```python
import functools

import jax
import jax.numpy as jnp
import numpy as np
from jax import lax
from jax.experimental import pallas as pl
from jax.experimental.pallas import tpu as pltpu
from jax.sharding import PartitionSpec as P

STEPS = 12
MATS = 8
BLOCK = 4
MESH = pl.DeviceIdType.MESH
NX, NY, NZ = 16, 32, 128
PX = BLOCK + 1
PY = 16
XP, YP = NX + 2 * PX, NY + 2 * PY
DEEP = BLOCK
MSGS = BLOCK + 1
FREE_PLANES = 13
BLOCKS = STEPS // BLOCK
SLOTS = BLOCKS * MSGS
DIRS = ((-1, 0), (1, 0), (0, -1), (0, 1), (-1, 1), (1, 1), (-1, -1), (1, -1))
W, E, S, N, NW, NE, SW, SE = range(8)
OPPOSITE = (E, W, N, S, SE, SW, NE, NW)
TILES = (12, 12, 8, 8, 4, 4, 4, 4)
MID = (8, 8, 4, 4, 0, 0, 0, 0)


def after_z(a, lane):
    return jnp.where(lane < NZ - 1, pltpu.roll(a, NZ - 1, 2), 0.0)


def before_z(a, lane):
    return jnp.where(lane > 0, pltpu.roll(a, 1, 2), 0.0)


def update_h(e, h, x, planes, row, n):
    lane = lax.broadcasted_iota(jnp.int32, (planes, n, NZ), 2)
    xs, ahead, rows, up = pl.ds(x, planes), pl.ds(x + 1, planes), pl.ds(row, n), pl.ds(row + 1, n)
    e0, e1, e2 = (e[c, xs, rows] for c in range(3))
    c0 = (e[2, xs, up] - e2) - (after_z(e1, lane) - e1)
    c1 = (after_z(e0, lane) - e0) - (e[2, ahead, rows] - e2)
    c2 = (e[1, ahead, rows] - e1) - (e[0, xs, up] - e0)
    new = [h[c, xs, rows] - curl for c, curl in enumerate((c0, c1, c2))]
    for c in range(3):
        h[c, xs, rows] = new[c]


def update_e(e, h, k, j, amp, x, planes, row, n):
    lane = lax.broadcasted_iota(jnp.int32, (planes, n, NZ), 2)
    xs, behind, rows, down = pl.ds(x, planes), pl.ds(x - 1, planes), pl.ds(row, n), pl.ds(row - 1, n)
    krows = pl.ds(row - 8, n)
    h0, h1, h2 = (h[c, xs, rows] for c in range(3))
    c0 = (h2 - h[2, xs, down]) - (h1 - before_z(h1, lane))
    c1 = (h0 - before_z(h0, lane)) - (h2 - h[2, behind, rows])
    c2 = (h1 - h[1, behind, rows]) - (h0 - h[0, xs, down])
    xx, yy, zz, xy, xz, yz = (k[c, xs, krows] for c in range(6))
    new0 = e[0, xs, rows] + ((xx * c0 + xy * c1) + (xz * c2 - amp * j[0, xs, krows]))
    new1 = e[1, xs, rows] + ((xy * c0 + yy * c1) + (yz * c2 - amp * j[1, xs, krows]))
    new2 = e[2, xs, rows] + ((xz * c0 + yz * c1) + (zz * c2 - amp * j[2, xs, krows]))
    for c, new in enumerate((new0, new1, new2)):
        e[c, xs, rows] = new


def sweep(lo, hi, most, body):
    count = hi - lo
    parts = -(-count // most)
    while count % parts:
        parts += 1
    planes = count // parts
    if parts == 1:
        body(lo, planes)
    else:
        def one(i, c):
            body(lo + i * planes, planes)
            return c

        lax.fori_loop(0, parts, one, 0)


def kernel(e_in, m_in, ids_in, table, e_out, m_out, et, ht, ef, hf, kk, jj, ids, own_x, own_y, ring, amps, *rest):
    out, inn = rest[:8], rest[8:16]
    out_sem, in_sem, id_out, id_in = rest[16:]
    gx, gy = lax.axis_index("gx"), lax.axis_index("gy")
    last_x, last_y = lax.axis_size("gx") - 1, lax.axis_size("gy") - 1

    def there(d):
        dx, dy = DIRS[d]
        checks = []
        if dx:
            checks.append(gx > 0 if dx < 0 else gx < last_x)
        if dy:
            checks.append(gy > 0 if dy < 0 else gy < last_y)
        return functools.reduce(jnp.logical_and, checks)

    def device(d):
        return (gx + DIRS[d][0], gy + DIRS[d][1])

    for d in range(8):
        def clear(s, c, d=d):
            inn[d][s] = jnp.zeros((TILES[d], 8, NZ), jnp.float32)
            return c
        lax.fori_loop(0, SLOTS, clear, 0)

    def clear_planes(x, c):
        ids[x] = jnp.full((YP - 16, NZ), -1, jnp.int32)
        for a in (ef, hf):
            for comp in range(3):
                a[comp, x] = jnp.zeros((YP, NZ), jnp.float32)
        return c

    lax.fori_loop(0, XP, clear_planes, 0)

    def clear_source(x, c):
        for comp in range(3):
            jj[comp, x] = jnp.zeros((YP - 16, NZ), jnp.float32)
        return c

    lax.fori_loop(0, XP, clear_source, 0)
    for step in range(STEPS):
        amps[step] = np.float32(np.sin(np.float32(0.3 * (step + 1))))

    barrier = pltpu.get_barrier_semaphore()
    for d in range(8):
        @pl.when(there(d))
        def _(d=d):
            pl.semaphore_signal(barrier, inc=1, device_id=device(d), device_id_type=MESH)
    peers = sum(there(d).astype(jnp.int32) for d in range(8))
    pl.semaphore_wait(barrier, peers)

    def id_copy(d):
        dx, dy = DIRS[d]
        xs = pl.ds(0 if dx < 0 else NX - DEEP, DEEP) if dx else pl.ds(0, NX)
        ys = pl.ds(0 if dy < 0 else NY - 8, 8) if dy else pl.ds(0, NY)
        xd = pl.ds(PX + NX if dx < 0 else PX - DEEP, DEEP) if dx else pl.ds(PX, NX)
        yd = pl.ds(8 + NY if dy < 0 else 0, 8) if dy else pl.ds(8, NY)
        return pltpu.make_async_remote_copy(
            src_ref=ids_in.at[xs, ys],
            dst_ref=ids.at[xd, yd],
            send_sem=id_out.at[d],
            recv_sem=id_in.at[d],
            device_id=device(d),
            device_id_type=MESH,
        )

    for d in range(8):
        @pl.when(there(d))
        def _(d=d):
            id_copy(d).start()

    def parts(d, slot, first, last):
        mid, tiles = MID[d], TILES[d]
        pieces = []
        if mid and not (first and d in (E, N)) and not (last and d in (W, S)):
            pieces.append((0, pl.ds(0, mid), pl.ds(0, 8)))
        if not first and not (last and d == SW):
            pieces.append((1, pl.ds(mid, tiles - mid), pl.ds(0, DEEP)))
        return pieces

    def copies(d, slot, first, last):
        return [
            pltpu.make_async_remote_copy(
                src_ref=out[d].at[slot, ts, rows],
                dst_ref=inn[d].at[slot, ts, rows],
                send_sem=out_sem.at[d, which, slot],
                recv_sem=in_sem.at[d, which, slot],
                device_id=device(d),
                device_id_type=MESH,
            )
            for which, ts, rows in parts(d, slot, first, last)
        ]

    def send(slot, first=False, last=False):
        for d in range(8):
            if parts(d, slot, first, last):
                @pl.when(there(d))
                def _(d=d):
                    for copy in copies(d, slot, first, last):
                        copy.start()

    def receive(slot, first=False, last=False):
        for d in range(8):
            if parts(d, slot, first, last):
                @pl.when(there(OPPOSITE[d]))
                def _(d=d):
                    for copy in copies(d, slot, first, last):
                        copy.wait_recv()

    def sent(slot, first=False, last=False):
        for d in range(8):
            if parts(d, slot, first, last):
                @pl.when(there(d))
                def _(d=d):
                    for copy in copies(d, slot, first, last):
                        copy.wait_send()

    XA, XZ, YA, YZ = PX, PX + NX - 1, PY, PY + NY - 1

    def put_face(d, slot, at, a, comps, x):
        for i, c in enumerate(comps):
            out[d][slot, pl.ds(at + 4 * i, 4)] = a[c, x, pl.ds(YA, NY)].reshape(4, 8, NZ)

    def put_line(d, slot, at, a, comps, y):
        for i, c in enumerate(comps):
            out[d][slot, pl.ds(at + 2 * i, 2)] = a[c, pl.ds(XA, NX), y].reshape(2, 8, NZ)

    def put_piece_y(d, slot, at, a, x, top):
        for i, c in enumerate((1, 2)):
            out[d][slot, at + i] = a[c, x, pl.ds(YZ + 1 if top else YA - DEEP, 8)]

    def put_piece_x(d, slot, at, a, y, right):
        for i, c in enumerate((0, 2)):
            out[d][slot, at + i, pl.ds(0, DEEP)] = a[c, pl.ds(XZ + 1 if right else XA - DEEP, DEEP), y]

    def pack_e(slot, corners=True):
        put_face(W, slot, 0, ef, (1, 2), XA)
        put_line(S, slot, 0, ef, (0, 2), YA)
        for i, c in enumerate((1, 2)):
            own_x[slot, 2 + i] = ef[c, XZ + 1, pl.ds(YA, NY)]
        for i, c in enumerate((0, 2)):
            own_y[slot, 2 + i] = ef[c, pl.ds(XA, NX), YZ + 1]
        if corners:
            put_piece_x(W, slot, 10, ef, YZ + 1, False)
            put_piece_x(E, slot, 10, ef, YZ + 1, True)
            put_piece_y(S, slot, 6, ef, XZ + 1, False)
            put_piece_y(N, slot, 6, ef, XZ + 1, True)
            put_piece_y(NW, slot, 0, ef, XA, True)
            put_piece_y(SW, slot, 0, ef, XA, False)
            put_piece_x(SW, slot, 2, ef, YA, False)
            put_piece_x(SE, slot, 2, ef, YA, True)

    def pack_h(slot):
        put_face(E, slot, 0, hf, (1, 2), XZ)
        put_line(N, slot, 0, hf, (0, 2), YZ)
        for i, c in enumerate((1, 2)):
            own_x[slot, i] = hf[c, XA - 1, pl.ds(YA, NY)]
        for i, c in enumerate((0, 2)):
            own_y[slot, i] = hf[c, pl.ds(XA, NX), YA - 1]
        put_piece_x(W, slot, 8, hf, YA - 1, False)
        put_piece_x(E, slot, 8, hf, YA - 1, True)
        put_piece_y(S, slot, 4, hf, XA - 1, False)
        put_piece_y(N, slot, 4, hf, XA - 1, True)
        put_piece_x(NW, slot, 2, hf, YZ, False)
        put_piece_y(NE, slot, 0, hf, XZ, True)
        put_piece_x(NE, slot, 2, hf, YZ, True)
        put_piece_y(SE, slot, 0, hf, XZ, False)

    def ring_x(a, x, slot, own, face, low, high):
        for i, c in enumerate((1, 2)):
            d, at = face
            a[c, x, pl.ds(YA, NY)] = own_x[slot, own + i] + inn[d][slot, pl.ds(at + 4 * i, 4)].reshape(NY, NZ)
            for pieces, row in ((low, YA), (high, YA + NY - DEEP)):
                (d1, at1), (d2, at2) = pieces
                a[c, x, pl.ds(row, 8)] = a[c, x, pl.ds(row, 8)] + (inn[d1][slot, at1 + i] + inn[d2][slot, at2 + i])

    def ring_y(a, y, slot, own, face, low, high):
        for i, c in enumerate((0, 2)):
            d, at = face
            ring[pl.ds(0, NX)] = own_y[slot, own + i] + inn[d][slot, pl.ds(at + 2 * i, 2)].reshape(NX, NZ)
            for pieces, row in ((low, 0), (high, NX - DEEP)):
                (d1, at1), (d2, at2) = pieces
                ring[pl.ds(row, 8)] = ring[pl.ds(row, 8)] + (inn[d1][slot, at1 + i] + inn[d2][slot, at2 + i])
            a[c, pl.ds(XA, NX), y] = ring[pl.ds(0, NX)]

    def ring_e(slot):
        ring_x(et, XZ + 1, slot, 2, (W, 0), ((N, 6), (NW, 0)), ((S, 6), (SW, 0)))
        ring_y(et, YZ + 1, slot, 2, (S, 0), ((E, 10), (SE, 2)), ((W, 10), (SW, 2)))

    def ring_h(slot):
        ring_x(ht, XA - 1, slot, 0, (E, 0), ((N, 4), (NE, 0)), ((S, 4), (SE, 0)))
        ring_y(ht, YA - 1, slot, 0, (N, 0), ((E, 8), (NE, 2)), ((W, 8), (NW, 2)))

    def look(x, row, n, source):
        here = ids[x, pl.ds(row, n)]
        bits = [(here & (1 << b)) != 0 for b in range(3)]
        real = here >= 0

        def pick(c):
            level = [table[m, c] for m in range(MATS)]
            for b in range(3):
                level = [jnp.where(bits[b], level[2 * i + 1], level[2 * i]) for i in range(len(level) // 2)]
            return level[0]

        tensor = [jnp.where(real, 0.2025 * pick(c), 0.0) for c in range(6)]
        for c in range(6):
            kk[c, x, pl.ds(row, n)] = tensor[c]
        if source:
            xx, yy, zz, xy, xz, yz = tensor
            s0, s1, s2 = ((1 / 0.45) * pick(c) for c in (6, 7, 8))
            jj[0, x, pl.ds(row, n)] = xx * s0 + xy * s1 + xz * s2
            jj[1, x, pl.ds(row, n)] = xy * s0 + yy * s1 + yz * s2
            jj[2, x, pl.ds(row, n)] = xz * s0 + yz * s1 + zz * s2

    def load(x, c):
        ids[x + PX, pl.ds(8, NY)] = ids_in[x]
        for comp in range(3):
            et[comp, x + PX, pl.ds(PY, NY)] = e_in[comp, x]
            ht[comp, x + PX, pl.ds(PY, NY)] = m_in[comp, x] * (1 / 0.45)
        return c

    lax.fori_loop(0, NX, load, 0)
    def look_own(x, c):
        look(x, 8, NY, True)
        return c

    def look_rows(x, c):
        look(x, 0, 8, False)
        look(x, 8 + NY, 8, False)
        return c

    def look_planes(x, c):
        look(x, 0, NY + 16, False)
        return c

    def block(b, c):
        base = b * MSGS

        def copy_in(x, c):
            for comp in range(3):
                for a, t in ((ef, et), (hf, ht)):
                    a[comp, x, pl.ds(8, 8)] = jnp.zeros((8, NZ), jnp.float32)
                    a[comp, x, pl.ds(PY, NY)] = t[comp, x, pl.ds(PY, NY)]
                    a[comp, x, pl.ds(PY + NY, 8)] = jnp.zeros((8, NZ), jnp.float32)
            return c

        def zero_plane(x, c):
            for comp in range(3):
                for a in (ef, hf):
                    a[comp, x, pl.ds(8, NY + 16)] = jnp.zeros((NY + 16, NZ), jnp.float32)
            return c

        lax.fori_loop(PX, PX + NX, copy_in, 0)

        @pl.when(b > 0)
        def _():
            lax.fori_loop(0, PX, zero_plane, 0)
            lax.fori_loop(PX + NX, XP, zero_plane, 0)

        pack_e(base, corners=False)
        send(base, first=True)

        @pl.when(b == 0)
        def _():
            lax.fori_loop(PX, PX + NX, look_own, 0)
            for d in range(8):
                @pl.when(there(OPPOSITE[d]))
                def _(d=d):
                    id_copy(d).wait_recv()
            lax.fori_loop(PX, PX + NX, look_rows, 0)
            lax.fori_loop(PX - DEEP, PX, look_planes, 0)
            lax.fori_loop(PX + NX, PX + NX + DEEP, look_planes, 0)

        def free_h(lo, hi):
            sweep(lo, hi, FREE_PLANES, lambda x, planes: update_h(ef, hf, x, planes, 8, NY + 16))

            @pl.when(gx == 0)
            def _():
                for comp in range(3):
                    hf[comp, PX - 1, pl.ds(8, NY + 16)] = jnp.zeros((NY + 16, NZ), jnp.float32)

            @pl.when(gy == 0)
            def _():
                for comp in range(3):
                    hf[comp, pl.ds(lo, hi - lo), pl.ds(8, 8)] = jnp.zeros((hi - lo, 8, NZ), jnp.float32)

        def free(t, c):
            amp = amps[b * BLOCK + t - 1]
            lo, hi = PX - (BLOCK - 1), PX + NX + BLOCK - 1
            free_h(lo, hi)
            sweep(lo, hi, FREE_PLANES, lambda x, planes: update_e(ef, hf, kk, jj, amp, x, planes, 8, NY + 16))
            pack_e(base + t)
            pack_h(base + t)
            send(base + t)
            return c

        lax.fori_loop(1, BLOCK, free, 0)
        free_h(PX - BLOCK, PX + NX + BLOCK - 1)
        pack_h(base + BLOCK)
        send(base + BLOCK, last=True)

        receive(base, first=True)

        def true_step(t):
            amp = amps[b * BLOCK + t - 1]
            ring_e(base + t - 1)
            ring_h(base + t)

            update_h(et, ht, PX, NX, PY, NY)
            update_e(et, ht, kk, jj, amp, PX, NX, PY, NY)

        def true(t, c):
            receive(base + t)
            true_step(t)
            return c

        lax.fori_loop(1, BLOCK, true, 0)
        receive(base + BLOCK, last=True)
        true_step(BLOCK)
        return c

    lax.fori_loop(0, BLOCKS, block, 0)

    def store(x, c):
        for comp in range(3):
            e_out[comp, x] = et[comp, x + PX, pl.ds(PY, NY)]
            m_out[comp, x] = ht[comp, x + PX, pl.ds(PY, NY)] * 0.45
        return c

    lax.fori_loop(0, NX, store, 0)

    for d in range(8):
        @pl.when(there(d))
        def _(d=d):
            id_copy(d).wait_send()

    def drain(b, c):
        sent(b * MSGS, first=True)

        def one(t, c):
            sent(b * MSGS + t)
            return c

        lax.fori_loop(1, BLOCK, one, 0)
        sent(b * MSGS + BLOCK, last=True)
        return c

    lax.fori_loop(0, BLOCKS, drain, 0)


def shards(electric, magnetic, material_ids, material_table):
    field = jax.ShapeDtypeStruct((3, NX, NY, NZ), jnp.float32)
    vmem = pl.BlockSpec(memory_space=pltpu.VMEM)
    big = pltpu.VMEM((3, XP, YP, NZ), jnp.float32)
    messages = [pltpu.VMEM((SLOTS, TILES[d], 8, NZ), jnp.float32) for d in range(8)]
    return pl.pallas_call(
        kernel,
        out_shape=(field, field),
        in_specs=[vmem, vmem, vmem, pl.BlockSpec(memory_space=pltpu.SMEM)],
        out_specs=(vmem, vmem),
        scratch_shapes=[
            big,
            big,
            big,
            big,
            pltpu.VMEM((6, XP, YP - 16, NZ), jnp.float32),
            pltpu.VMEM((3, XP, YP - 16, NZ), jnp.float32),
            pltpu.VMEM((XP, YP - 16, NZ), jnp.int32),
            pltpu.VMEM((SLOTS, 4, NY, NZ), jnp.float32),
            pltpu.VMEM((SLOTS, 4, NX, NZ), jnp.float32),
            pltpu.VMEM((NX + 8, NZ), jnp.float32),
            pltpu.SMEM((STEPS,), jnp.float32),
            *messages,
            *messages,
            pltpu.SemaphoreType.DMA((8, 2, SLOTS)),
            pltpu.SemaphoreType.DMA((8, 2, SLOTS)),
            pltpu.SemaphoreType.DMA((8,)),
            pltpu.SemaphoreType.DMA((8,)),
        ],
        compiler_params=pltpu.CompilerParams(
            collective_id=0, has_side_effects=True, vmem_limit_bytes=56 * 1024 * 1024
        ),
    )(electric, magnetic, material_ids, material_table)


def solution(mesh):
    placed = (P(None, "gx", "gy", None), P(None, "gx", "gy", None), P("gx", "gy", None), P())
    return jax.shard_map(
        shards,
        mesh=mesh,
        in_specs=placed,
        out_specs=(P(None, "gx", "gy", None), P(None, "gx", "gy", None)),
        check_vma=False,
    )
```

profile of v0, /device:TPU:57, one launch (start us, length us, event | category | flops | bytes accessed | tf_op | source)
XLA Modules:
  0.0 66.7 jit_solution(3015206754017863605)
XLA Ops:
  0.6 63.0 %shard_map.59 = (f32[3,16,32,128]{3,2,1,0:T(8,128)}, f32[3,16,32,128]{3,2,1,0:T(8,128)}) custom-call(f32[3,16,32,128]{3,2,1,0:T(8,128)} %e_in.1, f32[3,16,32,128]{3,2,1,0:T(8,128)} %m_in.1, s32[16,32,128]{2,1,0:T(8,128)} %ids_in.1, f32[8,9]{1,0:T(8,128)} %table.1), custom_call_target="tpu_custom_call" | custom-call | tf_op jit(solution)/shard_map/pallas_call | solution.py:437
  63.6 0.0 copy-start
  63.6 2.1 %copy.8 = f32[3,16,32,128]{3,2,1,0:T(8,128)} copy(f32[3,16,32,128]{3,2,1,0:T(8,128)} %get-tuple-element.4) | data formatting | bytes 1572864
  65.8 0.0 copy-done
  65.8 0.9 %copy.9 = f32[3,16,32,128]{3,2,1,0:T(8,128)} copy(f32[3,16,32,128]{3,2,1,0:T(8,128)S(1)} %copy-done) | data formatting | bytes 1572864
Async XLA Ops:
  63.6 2.1 %copy-start = (f32[3,16,32,128]{3,2,1,0:T(8,128)S(1)}, f32[3,16,32,128]{3,2,1,0:T(8,128)}, u32[]{:S(2)}) copy-start(f32[3,16,32,128]{3,2,1,0:T(8,128)} %get-tuple-element.5) | copy-start | bytes 2359300
where the time goes:
time: 67.6 us; the launch traced here: 66.7 us
  Pallas kernels  63 us (93%)
  local copies, waits for them, and re-layouts  3.02 us (4%)
    pallas_call x1, Pallas kernels, shards(): pl.pallas_call(kernel, out_shape=(field, field), in_specs=[vmem, vmem, vm...  63 us
    unnamed x4, local copies, waits for them, and re-layouts  3.02 us

commit v1 on v0

v1 whole, which is shorter than its diff:
```python
import functools

import jax
import jax.numpy as jnp
import numpy as np
from jax import lax
from jax.experimental import pallas as pl
from jax.experimental.pallas import tpu as pltpu
from jax.sharding import PartitionSpec as P

STEPS = 12
MATS = 8
BLOCK = 6
MESH = pl.DeviceIdType.MESH
NX, NY, NZ = 16, 32, 128
PX = BLOCK + 1
PY = 16
XP, YP = NX + 2 * PX, NY + 2 * PY
DEEP = BLOCK
IDS = BLOCK - 1
SLOTS = 2 + 6 + 7
DIRS = ((-1, 0), (1, 0), (0, -1), (0, 1), (-1, 1), (1, 1), (-1, -1), (1, -1))
W, E, S, N, NW, NE, SW, SE = range(8)
OPPOSITE = (E, W, N, S, SE, SW, NE, NW)
TILES = (12, 12, 8, 8, 4, 4, 4, 4)
MID = (8, 8, 4, 4, 0, 0, 0, 0)


def after_z(a, lane):
    return jnp.where(lane < NZ - 1, pltpu.roll(a, NZ - 1, 2), 0.0)


def before_z(a, lane):
    return jnp.where(lane > 0, pltpu.roll(a, 1, 2), 0.0)


def update_h(e, h, x, planes, row, n):
    lane = lax.broadcasted_iota(jnp.int32, (planes, n, NZ), 2)
    xs, ahead, rows, up = pl.ds(x, planes), pl.ds(x + 1, planes), pl.ds(row, n), pl.ds(row + 1, n)
    e0, e1, e2 = (e[c, xs, rows] for c in range(3))
    c0 = (e[2, xs, up] - e2) - (after_z(e1, lane) - e1)
    c1 = (after_z(e0, lane) - e0) - (e[2, ahead, rows] - e2)
    c2 = (e[1, ahead, rows] - e1) - (e[0, xs, up] - e0)
    new = [h[c, xs, rows] - 0.45 * curl for c, curl in enumerate((c0, c1, c2))]
    for c in range(3):
        h[c, xs, rows] = new[c]


def update_e(e, h, k, j, amp, x, planes, row, n):
    lane = lax.broadcasted_iota(jnp.int32, (planes, n, NZ), 2)
    xs, behind, rows, down = pl.ds(x, planes), pl.ds(x - 1, planes), pl.ds(row, n), pl.ds(row - 1, n)
    krows = pl.ds(row - 8, n)
    h0, h1, h2 = (h[c, xs, rows] for c in range(3))
    c0 = (h2 - h[2, xs, down]) - (h1 - before_z(h1, lane))
    c1 = (h0 - before_z(h0, lane)) - (h2 - h[2, behind, rows])
    c2 = (h1 - h[1, behind, rows]) - (h0 - h[0, xs, down])
    xx, yy, zz, xy, xz, yz = (k[c, xs, krows] for c in range(6))
    new0 = e[0, xs, rows] + ((xx * c0 + xy * c1) + (xz * c2 - amp * j[0, xs, krows]))
    new1 = e[1, xs, rows] + ((xy * c0 + yy * c1) + (yz * c2 - amp * j[1, xs, krows]))
    new2 = e[2, xs, rows] + ((xz * c0 + yz * c1) + (zz * c2 - amp * j[2, xs, krows]))
    for c, new in enumerate((new0, new1, new2)):
        e[c, xs, rows] = new


def kernel(e_in, m_in, ids_in, table, e_out, m_out, et, ht, ef, hf, kk, jj, ids, own_x, own_y, ring, amps, *rest):
    out, inn = rest[:8], rest[8:16]
    out_sem, in_sem, id_out, id_in, local = rest[16:]
    gx, gy = lax.axis_index("gx"), lax.axis_index("gy")
    last_x, last_y = lax.axis_size("gx") - 1, lax.axis_size("gy") - 1

    def there(d):
        dx, dy = DIRS[d]
        checks = []
        if dx:
            checks.append(gx > 0 if dx < 0 else gx < last_x)
        if dy:
            checks.append(gy > 0 if dy < 0 else gy < last_y)
        return functools.reduce(jnp.logical_and, checks)

    def device(d):
        return (gx + DIRS[d][0], gy + DIRS[d][1])

    box = (pl.ds(PX, NX), pl.ds(PY, NY))

    def load(i):
        pairs = [(ids_in, ids.at[pl.ds(PX, NX), pl.ds(8, NY)])]
        for comp in range(3):
            pairs.append((e_in.at[comp], et.at[(comp, *box)]))
            pairs.append((m_in.at[comp], ht.at[(comp, *box)]))
        return pltpu.make_async_copy(*pairs[i], local.at[i])

    for i in range(7):
        load(i).start()
    def clear_pieces(slot, c):
        for d in range(8):
            mid, tiles = MID[d], TILES[d]
            inn[d][slot, pl.ds(mid, tiles - mid)] = jnp.zeros((tiles - mid, 8, NZ), jnp.float32)
        return c

    lax.fori_loop(0, SLOTS, clear_pieces, 0)
    barrier = pltpu.get_barrier_semaphore()
    for d in range(8):
        @pl.when(there(d))
        def _(d=d):
            pl.semaphore_signal(barrier, inc=1, device_id=device(d), device_id_type=MESH)
    def around(d):
        dx, dy = DIRS[d]
        xd = pl.ds(PX + NX if dx < 0 else PX - IDS, IDS) if dx else pl.ds(PX, NX)
        yd = pl.ds(8 + NY if dy < 0 else 8 - IDS, IDS) if dy else pl.ds(8, NY)
        return xd, yd

    def id_copy(d):
        xd, yd = around(d)
        dx, dy = DIRS[d]
        xs = pl.ds(0 if dx < 0 else NX - IDS, IDS) if dx else pl.ds(0, NX)
        ys = pl.ds(0 if dy < 0 else NY - IDS, IDS) if dy else pl.ds(0, NY)
        return pltpu.make_async_remote_copy(
            src_ref=ids_in.at[xs, ys],
            dst_ref=ids.at[xd, yd],
            send_sem=id_out.at[d],
            recv_sem=id_in.at[d],
            device_id=device(d),
            device_id_type=MESH,
        )

    for d in range(8):
        @pl.when(jnp.logical_not(there(OPPOSITE[d])))
        def _(d=d):
            xd, yd = around(d)
            ids[xd, yd] = jnp.full((xd.size, yd.size, NZ), -1, jnp.int32)

            if MID[d]:
                def clear(s, c):
                    inn[d][s, pl.ds(0, MID[d])] = jnp.zeros((MID[d], 8, NZ), jnp.float32)
                    return c

                lax.fori_loop(0, SLOTS, clear, 0)

    def clear_planes(x, c):
        for comp in range(3):
            jj[comp, x] = jnp.zeros((YP - 16, NZ), jnp.float32)
            for a in (ef, hf):
                a[comp, x] = jnp.zeros((YP, NZ), jnp.float32)
        return c

    lax.fori_loop(0, XP, clear_planes, 0)
    for step in range(STEPS):
        amps[step] = np.float32(np.sin(np.float32(0.3 * (step + 1))))

    def parts(d, depth, last):
        mid, pieces = MID[d], []
        before, after = pl.ds(DEEP - depth, depth), pl.ds(0, depth)
        if mid and not (depth == 0 and d in (E, N)) and not (last and d in (W, S)):
            pieces.append((pl.ds(0, mid), pl.ds(0, 8)))
        if depth:
            if mid:
                pieces.append((pl.ds(mid, 2 if last else 4), before if d in (W, S) else after))
            if d in (NW, SE):
                pieces.append((pl.ds(0, 2), before))
                if not last:
                    pieces.append((pl.ds(2, 2), after))
            if d == NE:
                pieces.append((pl.ds(0, 4), after))
            if d == SW and not last:
                pieces.append((pl.ds(0, 4), before))
        return pieces

    def each(do, slot, depth, last, sending):
        for d in range(8):
            pieces = parts(d, depth, last)
            if pieces:
                @pl.when(there(d if sending else OPPOSITE[d]))
                def _(d=d):
                    for which, (ts, rows) in enumerate(pieces):
                        do(pltpu.make_async_remote_copy(
                            src_ref=out[d].at[slot, ts, rows],
                            dst_ref=inn[d].at[slot, ts, rows],
                            send_sem=out_sem.at[d, which, slot],
                            recv_sem=in_sem.at[d, which, slot],
                            device_id=device(d),
                            device_id_type=MESH,
                        ))

    def each_of(depths, do, slot, depth, last, sending):
        for m in depths:
            @pl.when(depth == m)
            def _(m=m):
                each(do, slot, m, last, sending)

    def start(copy):
        copy.start()

    def arrive(copy):
        copy.wait_recv()

    def leave(copy):
        copy.wait_send()

    XA, XZ, YA, YZ = PX, PX + NX - 1, PY, PY + NY - 1

    def put_face(d, slot, at, a, comps, x):
        for i, c in enumerate(comps):
            out[d][slot, pl.ds(at + 4 * i, 4)] = a[c, x, pl.ds(YA, NY)].reshape(4, 8, NZ)

    def put_line(d, slot, at, a, comps, y):
        for i, c in enumerate(comps):
            out[d][slot, pl.ds(at + 2 * i, 2)] = a[c, pl.ds(XA, NX), y].reshape(2, 8, NZ)

    def put_piece_y(d, slot, at, a, x, top):
        for i, c in enumerate((1, 2)):
            out[d][slot, at + i] = a[c, x, pl.ds(YZ + 1 if top else YA - DEEP, 8)]

    def put_piece_x(d, slot, at, a, y, right):
        for i, c in enumerate((0, 2)):
            out[d][slot, at + i, pl.ds(0, DEEP)] = a[c, pl.ds(XZ + 1 if right else XA - DEEP, DEEP), y]

    def pack_e(slot, corners=True):
        put_face(W, slot, 0, ef, (1, 2), XA)
        put_line(S, slot, 0, ef, (0, 2), YA)
        for i, c in enumerate((1, 2)):
            own_x[slot, 2 + i] = ef[c, XZ + 1, pl.ds(YA, NY)]
        for i, c in enumerate((0, 2)):
            own_y[slot, 2 + i] = ef[c, pl.ds(XA, NX), YZ + 1]
        if corners:
            put_piece_x(W, slot, 10, ef, YZ + 1, False)
            put_piece_x(E, slot, 10, ef, YZ + 1, True)
            put_piece_y(S, slot, 6, ef, XZ + 1, False)
            put_piece_y(N, slot, 6, ef, XZ + 1, True)
            put_piece_y(NW, slot, 2, ef, XA, True)
            put_piece_y(SW, slot, 0, ef, XA, False)
            put_piece_x(SW, slot, 2, ef, YA, False)
            put_piece_x(SE, slot, 2, ef, YA, True)

    def pack_h(slot):
        put_face(E, slot, 0, hf, (1, 2), XZ)
        put_line(N, slot, 0, hf, (0, 2), YZ)
        for i, c in enumerate((1, 2)):
            own_x[slot, i] = hf[c, XA - 1, pl.ds(YA, NY)]
        for i, c in enumerate((0, 2)):
            own_y[slot, i] = hf[c, pl.ds(XA, NX), YA - 1]
        put_piece_x(W, slot, 8, hf, YA - 1, False)
        put_piece_x(E, slot, 8, hf, YA - 1, True)
        put_piece_y(S, slot, 4, hf, XA - 1, False)
        put_piece_y(N, slot, 4, hf, XA - 1, True)
        put_piece_x(NW, slot, 0, hf, YZ, False)
        put_piece_y(NE, slot, 0, hf, XZ, True)
        put_piece_x(NE, slot, 2, hf, YZ, True)
        put_piece_y(SE, slot, 0, hf, XZ, False)

    def ring_x(a, x, slot, own, face, low, high):
        for i, c in enumerate((1, 2)):
            d, at = face
            a[c, x, pl.ds(YA, NY)] = own_x[slot, own + i] + inn[d][slot, pl.ds(at + 4 * i, 4)].reshape(NY, NZ)
            for pieces, row in ((low, YA), (high, YA + NY - DEEP)):
                (d1, at1), (d2, at2) = pieces
                some = pl.ds(0, DEEP)
                a[c, x, pl.ds(row, DEEP)] += inn[d1][slot, at1 + i, some] + inn[d2][slot, at2 + i, some]

    def ring_y(a, y, slot, own, face, low, high):
        for i, c in enumerate((0, 2)):
            d, at = face
            ring[...] = own_y[slot, own + i] + inn[d][slot, pl.ds(at + 2 * i, 2)].reshape(NX, NZ)
            for pieces, row in ((low, 0), (high, NX - DEEP)):
                (d1, at1), (d2, at2) = pieces
                some = pl.ds(0, DEEP)
                ring[pl.ds(row, DEEP)] += inn[d1][slot, at1 + i, some] + inn[d2][slot, at2 + i, some]
            a[c, pl.ds(XA, NX), y] = ring[...]

    def ring_e(slot):
        ring_x(et, XZ + 1, slot, 2, (W, 0), ((N, 6), (NW, 2)), ((S, 6), (SW, 0)))
        ring_y(et, YZ + 1, slot, 2, (S, 0), ((E, 10), (SE, 2)), ((W, 10), (SW, 2)))

    def ring_h(slot):
        ring_x(ht, XA - 1, slot, 0, (E, 0), ((N, 4), (NE, 0)), ((S, 4), (SE, 0)))
        ring_y(ht, YA - 1, slot, 0, (N, 0), ((E, 8), (NE, 2)), ((W, 8), (NW, 0)))

    def look(x, planes, row, n, source):
        xs, rows = pl.ds(x, planes), pl.ds(row, n)
        here = ids[xs, rows]
        bits = [(here & (1 << b)) != 0 for b in range(3)]
        real = here >= 0

        def pick(c):
            level = [table[m, c] for m in range(MATS)]
            for b in range(3):
                level = [jnp.where(bits[b], level[2 * i + 1], level[2 * i]) for i in range(len(level) // 2)]
            return level[0]

        tensor = [jnp.where(real, 0.45 * pick(c), 0.0) for c in range(6)]
        for c in range(6):
            kk[c, xs, rows] = tensor[c]
        if source:
            xx, yy, zz, xy, xz, yz = tensor
            s0, s1, s2 = (pick(c) for c in (6, 7, 8))
            jj[0, xs, rows] = xx * s0 + xy * s1 + xz * s2
            jj[1, xs, rows] = xy * s0 + yy * s1 + yz * s2
            jj[2, xs, rows] = xz * s0 + yz * s1 + zz * s2

    def look_own(i, c):
        look(PX + 2 * i, 2, 8, NY, True)
        return c

    def look_rows(i, c):
        look(PX + 4 * i, 4, 0, 8, False)
        look(PX + 4 * i, 4, 8 + NY, 8, False)
        return c

    def look_planes(i, c):
        look(PX - IDS + i, 1, 0, NY + 16, False)
        look(PX + NX + i, 1, 0, NY + 16, False)
        return c

    def frame(update):
        wide, halo = BLOCK - 1, BLOCK // 2
        update(PX - wide, NX + 2 * wide, 8, 16)
        update(PX - wide, NX + 2 * wide, 40, 16)
        update(PX - halo - 1, halo + BLOCK, 24, 16)
        update(PX + NX - BLOCK, halo + BLOCK, 24, 16)

    def lines_h(update):
        update(PX - BLOCK, NX + 2 * BLOCK, 8, 8)
        update(PX - BLOCK, NX + 2 * BLOCK, 40, 8)
        for x in (PX - 1, PX + NX - 1):
            update(x, 1, 16, 24)
            update(x, 1, 48, 8)

    def copy_in(i, c):
        xs = pl.ds(PX + 2 * i, 2)
        for comp in range(3):
            for a, t in ((ef, et), (hf, ht)):
                a[comp, xs, pl.ds(8, 8)] = jnp.zeros((2, 8, NZ), jnp.float32)
                a[comp, xs, pl.ds(PY, NY)] = t[comp, xs, pl.ds(PY, NY)]
                a[comp, xs, pl.ds(PY + NY, 8)] = jnp.zeros((2, 8, NZ), jnp.float32)
        return c

    def zero_plane(x, c):
        for comp in range(3):
            for a in (ef, hf):
                a[comp, x, pl.ds(8, NY + 16)] = jnp.zeros((NY + 16, NZ), jnp.float32)
        return c

    def edges_h():
        @pl.when(gx == 0)
        def _():
            for comp in range(3):
                hf[comp, PX - 1, pl.ds(8, NY + 16)] = jnp.zeros((NY + 16, NZ), jnp.float32)

        @pl.when(gy == 0)
        def _():
            for comp in range(3):
                hf[comp, :, pl.ds(8, 8)] = jnp.zeros((XP, 8, NZ), jnp.float32)

    def true_step(step, slot):
        ring_e(slot - 1)
        ring_h(slot)
        update_h(et, ht, PX, NX, PY, NY)
        update_e(et, ht, kk, jj, amps[step], PX, NX, PY, NY)

    load(0).wait()
    lax.fori_loop(0, NX // 2, look_own, 0)
    for i in range(1, 7):
        load(i).wait()
    lax.fori_loop(0, NX // 2, copy_in, 0)
    pack_e(0, corners=False)
    lines_h(functools.partial(update_h, ef, hf))
    edges_h()
    pack_h(1)
    peers = sum(there(d).astype(jnp.int32) for d in range(8))
    pl.semaphore_wait(barrier, peers)
    each(start, 0, 0, False, True)
    each(start, 1, 1, True, True)
    for d in range(8):
        @pl.when(there(d))
        def _(d=d):
            id_copy(d).start()
    each(arrive, 0, 0, False, False)
    each(arrive, 1, 1, True, False)
    true_step(0, 1)
    for d in range(8):
        @pl.when(there(OPPOSITE[d]))
        def _(d=d):
            id_copy(d).wait_recv()
    lax.fori_loop(0, NX // 4, look_rows, 0)
    lax.fori_loop(0, IDS, look_planes, 0)

    def block(b, c):
        size, begin, base = 4 + b, 5 * b - 4, 6 * b - 4
        lax.fori_loop(0, NX // 2, copy_in, 0)
        lax.fori_loop(0, PX, zero_plane, 0)
        lax.fori_loop(PX + NX, XP, zero_plane, 0)
        pack_e(base, corners=False)
        each(start, base, 0, False, True)

        def free(t, c):
            frame(functools.partial(update_h, ef, hf))
            edges_h()
            frame(functools.partial(update_e, ef, hf, kk, jj, amps[begin + t - 1]))
            pack_e(base + t)
            pack_h(base + t)
            each_of(range(1, BLOCK), start, base + t, t, False, True)
            return c

        lax.fori_loop(1, size, free, 0)
        lines_h(functools.partial(update_h, ef, hf))
        edges_h()
        pack_h(base + size)
        each_of((BLOCK - 1, BLOCK), start, base + size, size, True, True)
        each(arrive, base, 0, False, False)

        def true(t, c):
            @pl.when(t < size)
            def _():
                each_of(range(1, BLOCK), arrive, base + t, t, False, False)

            @pl.when(t == size)
            def _():
                each_of((BLOCK - 1, BLOCK), arrive, base + t, t, True, False)

            true_step(begin + t - 1, base + t)
            return c

        lax.fori_loop(1, size + 1, true, 0)
        return c

    lax.fori_loop(1, 3, block, 0)

    def stores():
        pairs = [(a.at[(comp, *box)], o.at[comp]) for a, o in ((et, e_out), (ht, m_out)) for comp in range(3)]
        return [pltpu.make_async_copy(src, dst, local.at[1 + i]) for i, (src, dst) in enumerate(pairs)]

    for copy in stores():
        copy.start()

    for d in range(8):
        @pl.when(there(d))
        def _(d=d):
            id_copy(d).wait_send()

    each(leave, 0, 0, False, True)
    each(leave, 1, 1, True, True)

    def drain(b, c):
        size, base = 4 + b, 6 * b - 4
        each(leave, base, 0, False, True)

        def one(t, c):
            each_of(range(1, BLOCK), leave, base + t, t, False, True)
            return c

        lax.fori_loop(1, size, one, 0)
        each_of((BLOCK - 1, BLOCK), leave, base + size, size, True, True)
        return c

    lax.fori_loop(1, 3, drain, 0)
    for copy in stores():
        copy.wait()


def shards(electric, magnetic, material_ids, material_table):
    field = jax.ShapeDtypeStruct((3, NX, NY, NZ), jnp.float32)
    hbm = pl.BlockSpec(memory_space=pl.ANY)
    big = pltpu.VMEM((3, XP, YP, NZ), jnp.float32)
    messages = [pltpu.VMEM((SLOTS, TILES[d], 8, NZ), jnp.float32) for d in range(8)]
    return pl.pallas_call(
        kernel,
        out_shape=(field, field),
        in_specs=[hbm, hbm, hbm, pl.BlockSpec(memory_space=pltpu.SMEM)],
        out_specs=(hbm, hbm),
        scratch_shapes=[
            big,
            big,
            big,
            big,
            pltpu.VMEM((6, XP, YP - 16, NZ), jnp.float32),
            pltpu.VMEM((3, XP, YP - 16, NZ), jnp.float32),
            pltpu.VMEM((XP, YP - 16, NZ), jnp.int32),
            pltpu.VMEM((SLOTS, 4, NY, NZ), jnp.float32),
            pltpu.VMEM((SLOTS, 4, NX, NZ), jnp.float32),
            pltpu.VMEM((NX, NZ), jnp.float32),
            pltpu.SMEM((STEPS,), jnp.float32),
            *messages,
            *messages,
            pltpu.SemaphoreType.DMA((8, 2, SLOTS)),
            pltpu.SemaphoreType.DMA((8, 2, SLOTS)),
            pltpu.SemaphoreType.DMA((8,)),
            pltpu.SemaphoreType.DMA((8,)),
            pltpu.SemaphoreType.DMA((7,)),
        ],
        compiler_params=pltpu.CompilerParams(
            collective_id=0, has_side_effects=True, vmem_limit_bytes=56 * 1024 * 1024
        ),
    )(electric, magnetic, material_ids, material_table)


def solution(mesh):
    placed = (P(None, "gx", "gy", None), P(None, "gx", "gy", None), P("gx", "gy", None), P())
    return jax.shard_map(
        shards,
        mesh=mesh,
        in_specs=placed,
        out_specs=(P(None, "gx", "gy", None), P(None, "gx", "gy", None)),
        check_vma=False,
    )
```

time: 67.6 us -> 58.8 us (0.87)
  Pallas kernels: 63 us -> 54.2 us
    pallas_call x1, Pallas kernels: 63 us -> 54.2 us  [shards(): pl.pallas_call(kernel, out_shape=(field, field), in_specs=[hbm, hbm, hbm,...]
where the time goes in v1:
time: 58.8 us; the launch traced here: 57.9 us
  Pallas kernels  54.2 us (92%)
  local copies, waits for them, and re-layouts  3.02 us (5%)
  between operations  0.65 us (1%)
    pallas_call x1, Pallas kernels, shards(): pl.pallas_call(kernel, out_shape=(field, field), in_specs=[hbm, hbm, hbm,...  54.2 us
    unnamed x4, local copies, waits for them, and re-layouts  3.02 us

profile of v1, /device:TPU:57, one launch (start us, length us, event | category | flops | bytes accessed | tf_op | source)
XLA Modules:
  0.0 57.9 jit_solution(9210151697483908324)
XLA Ops:
  0.6 54.2 %shard_map.59 = (f32[3,16,32,128]{3,2,1,0:T(8,128)}, f32[3,16,32,128]{3,2,1,0:T(8,128)}) custom-call(f32[3,16,32,128]{3,2,1,0:T(8,128)} %e_in.1, f32[3,16,32,128]{3,2,1,0:T(8,128)} %m_in.1, s32[16,32,128]{2,1,0:T(8,128)} %ids_in.1, f32[8,9]{1,0:T(8,128)} %table.1), custom_call_target="tpu_custom_call" | custom-call | tf_op jit(solution)/shard_map/pallas_call | solution.py:464
  54.8 0.0 copy-start
  54.9 2.1 %copy.8 = f32[3,16,32,128]{3,2,1,0:T(8,128)} copy(f32[3,16,32,128]{3,2,1,0:T(8,128)} %get-tuple-element.4) | data formatting | bytes 1572864
  57.0 0.0 copy-done
  57.0 0.9 %copy.9 = f32[3,16,32,128]{3,2,1,0:T(8,128)} copy(f32[3,16,32,128]{3,2,1,0:T(8,128)S(1)} %copy-done) | data formatting | bytes 1572864
Async XLA Ops:
  54.8 2.1 %copy-start = (f32[3,16,32,128]{3,2,1,0:T(8,128)S(1)}, f32[3,16,32,128]{3,2,1,0:T(8,128)}, u32[]{:S(2)}) copy-start(f32[3,16,32,128]{3,2,1,0:T(8,128)} %get-tuple-element.5) | copy-start | bytes 2359300

commit v2 on v1

--- a/solution.py
+++ b/solution.py
@@ -18,6 +18,7 @@
 XP, YP = NX + 2 * PX, NY + 2 * PY
 DEEP = BLOCK
 IDS = BLOCK - 1
+SIZES = (1, 5, 6)
 SLOTS = 2 + 6 + 7
 DIRS = ((-1, 0), (1, 0), (0, -1), (0, 1), (-1, 1), (1, 1), (-1, -1), (1, -1))
 W, E, S, N, NW, NE, SW, SE = range(8)
@@ -62,7 +63,7 @@
         e[c, xs, rows] = new
 
 
-def kernel(e_in, m_in, ids_in, table, e_out, m_out, et, ht, ef, hf, kk, jj, ids, own_x, own_y, ring, amps, *rest):
+def kernel(e_in, m_in, ids_in, table, e_out, m_out, et, ht, ef, hf, kk, jj, ids, own_x, own_y, ring, total, amps, *rest):
     out, inn = rest[:8], rest[8:16]
     out_sem, in_sem, id_out, id_in, local = rest[16:]
     gx, gy = lax.axis_index("gx"), lax.axis_index("gy")
@@ -149,52 +150,71 @@
 
     def parts(d, depth, last):
         mid, pieces = MID[d], []
-        before, after = pl.ds(DEEP - depth, depth), pl.ds(0, depth)
+        before, after, less = pl.ds(DEEP - depth, depth), pl.ds(0, depth), pl.ds(0, depth - 1)
         if mid and not (depth == 0 and d in (E, N)) and not (last and d in (W, S)):
             pieces.append((pl.ds(0, mid), pl.ds(0, 8)))
         if depth:
             if mid:
-                pieces.append((pl.ds(mid, 2 if last else 4), before if d in (W, S) else after))
+                if d in (W, S):
+                    pieces.append((pl.ds(mid, 2 if last else 4), before))
+                else:
+                    if depth > 1:
+                        pieces.append((pl.ds(mid, 2), less))
+                    if not last:
+                        pieces.append((pl.ds(mid + 2, 2), after))
             if d in (NW, SE):
                 pieces.append((pl.ds(0, 2), before))
                 if not last:
                     pieces.append((pl.ds(2, 2), after))
-            if d == NE:
-                pieces.append((pl.ds(0, 4), after))
+            if d == NE and depth > 1:
+                pieces.append((pl.ds(0, 4), less))
             if d == SW and not last:
                 pieces.append((pl.ds(0, 4), before))
         return pieces
 
-    def each(do, slot, depth, last, sending):
+    def rows_of(d, depth, last):
+        return sum(ts.size * rows.size for ts, rows in parts(d, depth, last))
+
+    def start(slot, depth, last):
         for d in range(8):
-            pieces = parts(d, depth, last)
-            if pieces:
-                @pl.when(there(d if sending else OPPOSITE[d]))
+            if parts(d, depth, last):
+                @pl.when(there(d))
                 def _(d=d):
-                    for which, (ts, rows) in enumerate(pieces):
-                        do(pltpu.make_async_remote_copy(
+                    for ts, rows in parts(d, depth, last):
+                        pltpu.make_async_remote_copy(
                             src_ref=out[d].at[slot, ts, rows],
                             dst_ref=inn[d].at[slot, ts, rows],
-                            send_sem=out_sem.at[d, which, slot],
-                            recv_sem=in_sem.at[d, which, slot],
+                            send_sem=out_sem.at[d],
+                            recv_sem=in_sem.at[d, slot],
                             device_id=device(d),
                             device_id_type=MESH,
-                        ))
-
-    def each_of(depths, do, slot, depth, last, sending):
+                        ).start()
+
+    def all_of(rows, sem):
+        some = total.at[pl.ds(0, rows)]
+        return pltpu.make_async_copy(some, some, sem)
+
+    def arrive(slot, depth, last):
+        for d in range(8):
+            if parts(d, depth, last):
+                @pl.when(there(OPPOSITE[d]))
+                def _(d=d):
+                    all_of(rows_of(d, depth, last), in_sem.at[d, slot]).wait()
+
+    def leave():
+        for d in range(8):
+            @pl.when(there(d))
+            def _(d=d):
+                rows = 0
+                for size in SIZES:
+                    rows += sum(rows_of(d, m, m == size) for m in range(size + 1))
+                all_of(rows, out_sem.at[d]).wait()
+
+    def one_of(depths, do, slot, depth, last):
         for m in depths:
             @pl.when(depth == m)
             def _(m=m):
-                each(do, slot, m, last, sending)
-
-    def start(copy):
-        copy.start()
-
-    def arrive(copy):
-        copy.wait_recv()
-
-    def leave(copy):
-        copy.wait_send()
+                do(slot, m, last)
 
     XA, XZ, YA, YZ = PX, PX + NX - 1, PY, PY + NY - 1
 
@@ -214,22 +234,27 @@
         for i, c in enumerate((0, 2)):
             out[d][slot, at + i, pl.ds(0, DEEP)] = a[c, pl.ds(XZ + 1 if right else XA - DEEP, DEEP), y]
 
-    def pack_e(slot, corners=True):
+    def pack_first(slot):
+        put_face(W, slot, 0, et, (1, 2), XA)
+        put_line(S, slot, 0, et, (0, 2), YA)
+        own_x[slot, pl.ds(2, 2)] = jnp.zeros((2, NY, NZ), jnp.float32)
+        own_y[slot, pl.ds(2, 2)] = jnp.zeros((2, NX, NZ), jnp.float32)
+
+    def pack_e(slot):
         put_face(W, slot, 0, ef, (1, 2), XA)
         put_line(S, slot, 0, ef, (0, 2), YA)
         for i, c in enumerate((1, 2)):
             own_x[slot, 2 + i] = ef[c, XZ + 1, pl.ds(YA, NY)]
         for i, c in enumerate((0, 2)):
             own_y[slot, 2 + i] = ef[c, pl.ds(XA, NX), YZ + 1]
-        if corners:
-            put_piece_x(W, slot, 10, ef, YZ + 1, False)
-            put_piece_x(E, slot, 10, ef, YZ + 1, True)
-            put_piece_y(S, slot, 6, ef, XZ + 1, False)
-            put_piece_y(N, slot, 6, ef, XZ + 1, True)
-            put_piece_y(NW, slot, 2, ef, XA, True)
-            put_piece_y(SW, slot, 0, ef, XA, False)
-            put_piece_x(SW, slot, 2, ef, YA, False)
-            put_piece_x(SE, slot, 2, ef, YA, True)
+        put_piece_x(W, slot, 10, ef, YZ + 1, False)
+        put_piece_x(E, slot, 10, ef, YZ + 1, True)
+        put_piece_y(S, slot, 6, ef, XZ + 1, False)
+        put_piece_y(N, slot, 6, ef, XZ + 1, True)
+        put_piece_y(NW, slot, 2, ef, XA, True)
+        put_piece_y(SW, slot, 0, ef, XA, False)
+        put_piece_x(SW, slot, 2, ef, YA, False)
+        put_piece_x(SE, slot, 2, ef, YA, True)
 
     def pack_h(slot):
         put_face(E, slot, 0, hf, (1, 2), XZ)
@@ -337,6 +362,7 @@
         for comp in range(3):
             for a in (ef, hf):
                 a[comp, x, pl.ds(8, NY + 16)] = jnp.zeros((NY + 16, NZ), jnp.float32)
+                a[comp, x + PX + NX, pl.ds(8, NY + 16)] = jnp.zeros((NY + 16, NZ), jnp.float32)
         return c
 
     def edges_h():
@@ -361,60 +387,65 @@
     for i in range(1, 7):
         load(i).wait()
     lax.fori_loop(0, NX // 2, copy_in, 0)
-    pack_e(0, corners=False)
+    pack_first(0)
     lines_h(functools.partial(update_h, ef, hf))
     edges_h()
     pack_h(1)
     peers = sum(there(d).astype(jnp.int32) for d in range(8))
     pl.semaphore_wait(barrier, peers)
-    each(start, 0, 0, False, True)
-    each(start, 1, 1, True, True)
+    start(0, 0, False)
+    start(1, 1, True)
     for d in range(8):
         @pl.when(there(d))
         def _(d=d):
             id_copy(d).start()
-    each(arrive, 0, 0, False, False)
-    each(arrive, 1, 1, True, False)
+    arrive(0, 0, False)
+    arrive(1, 1, True)
     true_step(0, 1)
-    for d in range(8):
-        @pl.when(there(OPPOSITE[d]))
-        def _(d=d):
-            id_copy(d).wait_recv()
-    lax.fori_loop(0, NX // 4, look_rows, 0)
-    lax.fori_loop(0, IDS, look_planes, 0)
+    def look_around():
+        for d in range(8):
+            @pl.when(there(OPPOSITE[d]))
+            def _(d=d):
+                id_copy(d).wait_recv()
+        lax.fori_loop(0, NX // 4, look_rows, 0)
+        lax.fori_loop(0, IDS, look_planes, 0)
 
     def block(b, c):
         size, begin, base = 4 + b, 5 * b - 4, 6 * b - 4
+        pack_first(base)
+        start(base, 0, False)
         lax.fori_loop(0, NX // 2, copy_in, 0)
         lax.fori_loop(0, PX, zero_plane, 0)
-        lax.fori_loop(PX + NX, XP, zero_plane, 0)
-        pack_e(base, corners=False)
-        each(start, base, 0, False, True)
 
         def free(t, c):
             frame(functools.partial(update_h, ef, hf))
             edges_h()
+
+            @pl.when((b == 1) & (t == 1))
+            def _():
+                look_around()
+
             frame(functools.partial(update_e, ef, hf, kk, jj, amps[begin + t - 1]))
             pack_e(base + t)
             pack_h(base + t)
-            each_of(range(1, BLOCK), start, base + t, t, False, True)
+            one_of(range(1, BLOCK), start, base + t, t, False)
             return c
 
         lax.fori_loop(1, size, free, 0)
         lines_h(functools.partial(update_h, ef, hf))
         edges_h()
         pack_h(base + size)
-        each_of((BLOCK - 1, BLOCK), start, base + size, size, True, True)
-        each(arrive, base, 0, False, False)
+        one_of((BLOCK - 1, BLOCK), start, base + size, size, True)
+        arrive(base, 0, False)
 
         def true(t, c):
             @pl.when(t < size)
             def _():
-                each_of(range(1, BLOCK), arrive, base + t, t, False, False)
+                one_of(range(1, BLOCK), arrive, base + t, t, False)
 
             @pl.when(t == size)
             def _():
-                each_of((BLOCK - 1, BLOCK), arrive, base + t, t, True, False)
+                one_of((BLOCK - 1, BLOCK), arrive, base + t, t, True)
 
             true_step(begin + t - 1, base + t)
             return c
@@ -436,22 +467,7 @@
         def _(d=d):
             id_copy(d).wait_send()
 
-    each(leave, 0, 0, False, True)
-    each(leave, 1, 1, True, True)
-
-    def drain(b, c):
-        size, base = 4 + b, 6 * b - 4
-        each(leave, base, 0, False, True)
-
-        def one(t, c):
-            each_of(range(1, BLOCK), leave, base + t, t, False, True)
-            return c
-
-        lax.fori_loop(1, size, one, 0)
-        each_of((BLOCK - 1, BLOCK), leave, base + size, size, True, True)
-        return c
-
-    lax.fori_loop(1, 3, drain, 0)
+    leave()
     for copy in stores():
         copy.wait()
 
@@ -477,11 +493,12 @@
             pltpu.VMEM((SLOTS, 4, NY, NZ), jnp.float32),
             pltpu.VMEM((SLOTS, 4, NX, NZ), jnp.float32),
             pltpu.VMEM((NX, NZ), jnp.float32),
+            pltpu.VMEM((2048, NZ), jnp.float32),
             pltpu.SMEM((STEPS,), jnp.float32),
             *messages,
             *messages,
-            pltpu.SemaphoreType.DMA((8, 2, SLOTS)),
-            pltpu.SemaphoreType.DMA((8, 2, SLOTS)),
+            pltpu.SemaphoreType.DMA((8,)),
+            pltpu.SemaphoreType.DMA((8, SLOTS)),
             pltpu.SemaphoreType.DMA((8,)),
             pltpu.SemaphoreType.DMA((8,)),
             pltpu.SemaphoreType.DMA((7,)),

time: 58.8 us -> 54.2 us (0.922)
  Pallas kernels: 54.2 us -> 49.6 us
    pallas_call x1, Pallas kernels: 54.2 us -> 49.6 us  [shards(): pl.pallas_call(kernel, out_shape=(field, field), in_specs=[hbm, hbm, hbm,...]
where the time goes in v2:
time: 54.2 us; the launch traced here: 53.3 us
  Pallas kernels  49.6 us (92%)
  local copies, waits for them, and re-layouts  3.02 us (6%)
  between operations  0.65 us (1%)
    pallas_call x1, Pallas kernels, shards(): pl.pallas_call(kernel, out_shape=(field, field), in_specs=[hbm, hbm, hbm,...  49.6 us
    unnamed x4, local copies, waits for them, and re-layouts  3.02 us

profile of v2, /device:TPU:57, one launch (start us, length us, event | category | flops | bytes accessed | tf_op | source)
XLA Modules:
  0.0 53.3 jit_solution(17994852761901394293)
XLA Ops:
  0.6 49.6 %shard_map.59 = (f32[3,16,32,128]{3,2,1,0:T(8,128)}, f32[3,16,32,128]{3,2,1,0:T(8,128)}) custom-call(f32[3,16,32,128]{3,2,1,0:T(8,128)} %e_in.1, f32[3,16,32,128]{3,2,1,0:T(8,128)} %m_in.1, s32[16,32,128]{2,1,0:T(8,128)} %ids_in.1, f32[8,9]{1,0:T(8,128)} %table.1), custom_call_target="tpu_custom_call" | custom-call | tf_op jit(solution)/shard_map/pallas_call | solution.py:480
  50.2 0.0 copy-start
  50.2 2.1 %copy.8 = f32[3,16,32,128]{3,2,1,0:T(8,128)} copy(f32[3,16,32,128]{3,2,1,0:T(8,128)} %get-tuple-element.4) | data formatting | bytes 1572864
  52.4 0.0 copy-done
  52.4 0.9 %copy.9 = f32[3,16,32,128]{3,2,1,0:T(8,128)} copy(f32[3,16,32,128]{3,2,1,0:T(8,128)S(1)} %copy-done) | data formatting | bytes 1572864
Async XLA Ops:
  50.2 2.1 %copy-start = (f32[3,16,32,128]{3,2,1,0:T(8,128)S(1)}, f32[3,16,32,128]{3,2,1,0:T(8,128)}, u32[]{:S(2)}) copy-start(f32[3,16,32,128]{3,2,1,0:T(8,128)} %get-tuple-element.5) | copy-start | bytes 2359300

commit v3 on v2

--- a/solution.py
+++ b/solution.py
@@ -148,39 +148,38 @@
     for step in range(STEPS):
         amps[step] = np.float32(np.sin(np.float32(0.3 * (step + 1))))
 
+    def parts_h(d, depth):
+        mid, pieces = MID[d], []
+        before, less = pl.ds(DEEP - depth, depth), pl.ds(0, depth - 1)
+        if d in (E, N):
+            pieces.append((pl.ds(0, mid), pl.ds(0, 8)))
+        if d in (W, S, NW, SE):
+            pieces.append((pl.ds(mid, 2), before))
+        if d in (E, N, NE) and depth > 1:
+            pieces.append((pl.ds(mid, 4 if d == NE else 2), less))
+        return pieces
+
+    def parts_e(d, depth):
+        mid, pieces = MID[d], []
+        before, after = pl.ds(DEEP - depth, depth), pl.ds(0, depth)
+        if d in (W, S):
+            pieces.append((pl.ds(0, mid), pl.ds(0, 8)))
+        if depth and d != NE:
+            pieces.append((pl.ds(0, 4) if d == SW else pl.ds(mid + 2, 2), before if d in (W, S, SW) else after))
+        return pieces
+
     def parts(d, depth, last):
-        mid, pieces = MID[d], []
-        before, after, less = pl.ds(DEEP - depth, depth), pl.ds(0, depth), pl.ds(0, depth - 1)
-        if mid and not (depth == 0 and d in (E, N)) and not (last and d in (W, S)):
-            pieces.append((pl.ds(0, mid), pl.ds(0, 8)))
-        if depth:
-            if mid:
-                if d in (W, S):
-                    pieces.append((pl.ds(mid, 2 if last else 4), before))
-                else:
-                    if depth > 1:
-                        pieces.append((pl.ds(mid, 2), less))
-                    if not last:
-                        pieces.append((pl.ds(mid + 2, 2), after))
-            if d in (NW, SE):
-                pieces.append((pl.ds(0, 2), before))
-                if not last:
-                    pieces.append((pl.ds(2, 2), after))
-            if d == NE and depth > 1:
-                pieces.append((pl.ds(0, 4), less))
-            if d == SW and not last:
-                pieces.append((pl.ds(0, 4), before))
-        return pieces
+        return (parts_h(d, depth) if depth else []) + ([] if last else parts_e(d, depth))
 
     def rows_of(d, depth, last):
         return sum(ts.size * rows.size for ts, rows in parts(d, depth, last))
 
-    def start(slot, depth, last):
+    def start(slot, depth, some):
         for d in range(8):
-            if parts(d, depth, last):
+            if some(d, depth):
                 @pl.when(there(d))
                 def _(d=d):
-                    for ts, rows in parts(d, depth, last):
+                    for ts, rows in some(d, depth):
                         pltpu.make_async_remote_copy(
                             src_ref=out[d].at[slot, ts, rows],
                             dst_ref=inn[d].at[slot, ts, rows],
@@ -210,11 +209,11 @@
                     rows += sum(rows_of(d, m, m == size) for m in range(size + 1))
                 all_of(rows, out_sem.at[d]).wait()
 
-    def one_of(depths, do, slot, depth, last):
+    def one_of(depths, do, slot, depth, *what):
         for m in depths:
             @pl.when(depth == m)
             def _(m=m):
-                do(slot, m, last)
+                do(slot, m, *what)
 
     XA, XZ, YA, YZ = PX, PX + NX - 1, PY, PY + NY - 1
 
@@ -350,20 +349,29 @@
             update(x, 1, 48, 8)
 
     def copy_in(i, c):
-        xs = pl.ds(PX + 2 * i, 2)
+        xs, rows = pl.ds(PX + 4 * i, 4), pl.ds(PY, NY)
         for comp in range(3):
             for a, t in ((ef, et), (hf, ht)):
-                a[comp, xs, pl.ds(8, 8)] = jnp.zeros((2, 8, NZ), jnp.float32)
-                a[comp, xs, pl.ds(PY, NY)] = t[comp, xs, pl.ds(PY, NY)]
-                a[comp, xs, pl.ds(PY + NY, 8)] = jnp.zeros((2, 8, NZ), jnp.float32)
-        return c
-
-    def zero_plane(x, c):
+                a[comp, xs, rows] = t[comp, xs, rows]
+        return c
+
+    def clean_rows(i, c):
         for comp in range(3):
             for a in (ef, hf):
-                a[comp, x, pl.ds(8, NY + 16)] = jnp.zeros((NY + 16, NZ), jnp.float32)
-                a[comp, x + PX + NX, pl.ds(8, NY + 16)] = jnp.zeros((NY + 16, NZ), jnp.float32)
-        return c
+                for row in (8, PY + NY):
+                    a[comp, pl.ds(PX + 4 * i, 4), pl.ds(row, 8)] = jnp.zeros((4, 8, NZ), jnp.float32)
+        return c
+
+    def clean_plane(x, c):
+        for comp in range(3):
+            for a in (ef, hf):
+                for at in (x, x + PX + NX):
+                    a[comp, at, pl.ds(8, NY + 16)] = jnp.zeros((NY + 16, NZ), jnp.float32)
+        return c
+
+    def clean():
+        lax.fori_loop(0, NX // 4, clean_rows, 0)
+        lax.fori_loop(0, PX, clean_plane, 0)
 
     def edges_h():
         @pl.when(gx == 0)
@@ -376,32 +384,36 @@
             for comp in range(3):
                 hf[comp, :, pl.ds(8, 8)] = jnp.zeros((XP, 8, NZ), jnp.float32)
 
-    def true_step(step, slot):
+    def true_step(step, slot, wait):
+        some_e = functools.partial(update_e, et, ht, kk, jj, amps[step])
         ring_e(slot - 1)
+        update_h(et, ht, PX, NX, PY, NY)
+        some_e(PX + 1, NX - 1, PY + 8, NY - 8)
+        wait()
         ring_h(slot)
-        update_h(et, ht, PX, NX, PY, NY)
-        update_e(et, ht, kk, jj, amps[step], PX, NX, PY, NY)
+        some_e(PX, 1, PY, NY)
+        some_e(PX + 1, NX - 1, PY, 8)
 
     load(0).wait()
     lax.fori_loop(0, NX // 2, look_own, 0)
     for i in range(1, 7):
         load(i).wait()
-    lax.fori_loop(0, NX // 2, copy_in, 0)
+    lax.fori_loop(0, NX // 4, copy_in, 0)
     pack_first(0)
     lines_h(functools.partial(update_h, ef, hf))
     edges_h()
     pack_h(1)
     peers = sum(there(d).astype(jnp.int32) for d in range(8))
     pl.semaphore_wait(barrier, peers)
-    start(0, 0, False)
-    start(1, 1, True)
+    start(0, 0, parts_e)
+    start(1, 1, parts_h)
     for d in range(8):
         @pl.when(there(d))
         def _(d=d):
             id_copy(d).start()
+    clean()
     arrive(0, 0, False)
-    arrive(1, 1, True)
-    true_step(0, 1)
+    true_step(0, 1, functools.partial(arrive, 1, 1, True))
     def look_around():
         for d in range(8):
             @pl.when(there(OPPOSITE[d]))
@@ -413,13 +425,14 @@
     def block(b, c):
         size, begin, base = 4 + b, 5 * b - 4, 6 * b - 4
         pack_first(base)
-        start(base, 0, False)
-        lax.fori_loop(0, NX // 2, copy_in, 0)
-        lax.fori_loop(0, PX, zero_plane, 0)
+        start(base, 0, parts_e)
+        lax.fori_loop(0, NX // 4, copy_in, 0)
 
         def free(t, c):
             frame(functools.partial(update_h, ef, hf))
             edges_h()
+            pack_h(base + t)
+            one_of(range(1, BLOCK), start, base + t, t, parts_h)
 
             @pl.when((b == 1) & (t == 1))
             def _():
@@ -427,27 +440,28 @@
 
             frame(functools.partial(update_e, ef, hf, kk, jj, amps[begin + t - 1]))
             pack_e(base + t)
-            pack_h(base + t)
-            one_of(range(1, BLOCK), start, base + t, t, False)
+            one_of(range(1, BLOCK), start, base + t, t, parts_e)
             return c
 
         lax.fori_loop(1, size, free, 0)
         lines_h(functools.partial(update_h, ef, hf))
         edges_h()
         pack_h(base + size)
-        one_of((BLOCK - 1, BLOCK), start, base + size, size, True)
+        one_of((BLOCK - 1, BLOCK), start, base + size, size, parts_h)
+        clean()
         arrive(base, 0, False)
 
         def true(t, c):
-            @pl.when(t < size)
-            def _():
-                one_of(range(1, BLOCK), arrive, base + t, t, False)
-
-            @pl.when(t == size)
-            def _():
-                one_of((BLOCK - 1, BLOCK), arrive, base + t, t, True)
-
-            true_step(begin + t - 1, base + t)
+            def wait():
+                @pl.when(t < size)
+                def _():
+                    one_of(range(1, BLOCK), arrive, base + t, t, False)
+
+                @pl.when(t == size)
+                def _():
+                    one_of((BLOCK - 1, BLOCK), arrive, base + t, t, True)
+
+            true_step(begin + t - 1, base + t, wait)
             return c
 
         lax.fori_loop(1, size + 1, true, 0)
@@ -470,6 +484,19 @@
     leave()
     for copy in stores():
         copy.wait()
+
+
+def hand_over(e_in, m_in, e_out, m_out, held, in_sem, out_sem):
+    pairs = [(a.at[c], o.at[c]) for a, o in ((e_in, e_out), (m_in, m_out)) for c in range(3)]
+    loads = [pltpu.make_async_copy(a, held.at[i], in_sem.at[i]) for i, (a, _) in enumerate(pairs)]
+    stores = [pltpu.make_async_copy(held.at[i], o, out_sem.at[i]) for i, (_, o) in enumerate(pairs)]
+    for load in loads:
+        load.start()
+    for load, store in zip(loads, stores):
+        load.wait()
+        store.start()
+    for store in stores:
+        store.wait()
 
 
 def shards(electric, magnetic, material_ids, material_table):
@@ -477,7 +504,7 @@
     hbm = pl.BlockSpec(memory_space=pl.ANY)
     big = pltpu.VMEM((3, XP, YP, NZ), jnp.float32)
     messages = [pltpu.VMEM((SLOTS, TILES[d], 8, NZ), jnp.float32) for d in range(8)]
-    return pl.pallas_call(
+    e, m = pl.pallas_call(
         kernel,
         out_shape=(field, field),
         in_specs=[hbm, hbm, hbm, pl.BlockSpec(memory_space=pltpu.SMEM)],
@@ -507,6 +534,13 @@
             collective_id=0, has_side_effects=True, vmem_limit_bytes=56 * 1024 * 1024
         ),
     )(electric, magnetic, material_ids, material_table)
+    return pl.pallas_call(
+        hand_over,
+        out_shape=(field, field),
+        in_specs=[hbm, hbm],
+        out_specs=(hbm, hbm),
+        scratch_shapes=[pltpu.VMEM((6, NX, NY, NZ), jnp.float32), pltpu.SemaphoreType.DMA((6,)), pltpu.SemaphoreType.DMA((6,))],
+    )(e, m)
 
 
 def solution(mesh):

time: 54.2 us -> 50.7 us (0.935)
  local copies, waits for them, and re-layouts: 3.02 us -> 0 us
    unnamed x4 -> x0, local copies, waits for them, and re-layouts: 3.02 us -> none
    pallas_call x1, Pallas kernels: 49.6 us -> 47.2 us  [shards(): pl.pallas_call(kernel, out_shape=(field, field), in_specs=[hbm, hbm, hbm,...]
    pallas_call x0 -> x1, Pallas kernels: none -> 2.19 us  [shards(): pl.pallas_call(hand_over, out_shape=(field, field), in_specs=[hbm, hbm],...]
where the time goes in v3:
time: 50.7 us; the launch traced here: 50 us
  Pallas kernels  49.4 us (97%)
  between operations  0.64 us (1%)
    pallas_call x1, Pallas kernels, shards(): pl.pallas_call(kernel, out_shape=(field, field), in_specs=[hbm, hbm, hbm,...  47.2 us
    pallas_call x1, Pallas kernels, shards(): pl.pallas_call(hand_over, out_shape=(field, field), in_specs=[hbm, hbm],...  2.19 us

profile of v3, /device:TPU:57, one launch (start us, length us, event | category | flops | bytes accessed | tf_op | source)
XLA Modules:
  0.0 50.0 jit_solution(3960561482619652304)
XLA Ops:
  0.6 47.2 %shard_map.59 = (f32[3,16,32,128]{3,2,1,0:T(8,128)}, f32[3,16,32,128]{3,2,1,0:T(8,128)}) custom-call(f32[3,16,32,128]{3,2,1,0:T(8,128)} %e_in.1, f32[3,16,32,128]{3,2,1,0:T(8,128)} %m_in.1, s32[16,32,128]{2,1,0:T(8,128)} %ids_in.1, f32[8,9]{1,0:T(8,128)} %table.1), custom_call_target="tpu_custom_call" | custom-call | tf_op jit(solution)/shard_map/pallas_call | solution.py:507
  47.8 2.2 %shard_map.60 = (f32[3,16,32,128]{3,2,1,0:T(8,128)}, f32[3,16,32,128]{3,2,1,0:T(8,128)}) custom-call(f32[3,16,32,128]{3,2,1,0:T(8,128)} %get-tuple-element.4.e_in, f32[3,16,32,128]{3,2,1,0:T(8,128)} %get-tuple-element.5.m_in), custom_call_target="tpu_custom_call" | custom-call | tf_op jit(solution)/shard_map/pallas_call | solution.py:537

commit v4 on v3

--- a/solution.py
+++ b/solution.py
@@ -10,7 +10,7 @@
 
 STEPS = 12
 MATS = 8
-BLOCK = 6
+BLOCK = 4
 MESH = pl.DeviceIdType.MESH
 NX, NY, NZ = 16, 32, 128
 PX = BLOCK + 1
@@ -18,8 +18,9 @@
 XP, YP = NX + 2 * PX, NY + 2 * PY
 DEEP = BLOCK
 IDS = BLOCK - 1
-SIZES = (1, 5, 6)
-SLOTS = 2 + 6 + 7
+SIZES = (1, 3, 4, 4)
+SLOTS = 2 + 4 + 5 + 5
+TURNS = 2 * (BLOCK + 1)
 DIRS = ((-1, 0), (1, 0), (0, -1), (0, 1), (-1, 1), (1, 1), (-1, -1), (1, -1))
 W, E, S, N, NW, NE, SW, SE = range(8)
 OPPOSITE = (E, W, N, S, SE, SW, NE, NW)
@@ -174,7 +175,10 @@
     def rows_of(d, depth, last):
         return sum(ts.size * rows.size for ts, rows in parts(d, depth, last))
 
-    def start(slot, depth, some):
+    def turn(block, depth):
+        return lax.rem(block, 2) * (BLOCK + 1) + depth
+
+    def start(block, slot, depth, some):
         for d in range(8):
             if some(d, depth):
                 @pl.when(there(d))
@@ -184,7 +188,7 @@
                             src_ref=out[d].at[slot, ts, rows],
                             dst_ref=inn[d].at[slot, ts, rows],
                             send_sem=out_sem.at[d],
-                            recv_sem=in_sem.at[d, slot],
+                            recv_sem=in_sem.at[d, turn(block, depth)],
                             device_id=device(d),
                             device_id_type=MESH,
                         ).start()
@@ -193,12 +197,12 @@
         some = total.at[pl.ds(0, rows)]
         return pltpu.make_async_copy(some, some, sem)
 
-    def arrive(slot, depth, last):
+    def arrive(block, slot, depth, last):
         for d in range(8):
             if parts(d, depth, last):
                 @pl.when(there(OPPOSITE[d]))
                 def _(d=d):
-                    all_of(rows_of(d, depth, last), in_sem.at[d, slot]).wait()
+                    all_of(rows_of(d, depth, last), in_sem.at[d, turn(block, depth)]).wait()
 
     def leave():
         for d in range(8):
@@ -209,11 +213,11 @@
                     rows += sum(rows_of(d, m, m == size) for m in range(size + 1))
                 all_of(rows, out_sem.at[d]).wait()
 
-    def one_of(depths, do, slot, depth, *what):
+    def one_of(depths, do, block, slot, depth, *what):
         for m in depths:
             @pl.when(depth == m)
             def _(m=m):
-                do(slot, m, *what)
+                do(block, slot, m, *what)
 
     XA, XZ, YA, YZ = PX, PX + NX - 1, PY, PY + NY - 1
 
@@ -384,15 +388,20 @@
             for comp in range(3):
                 hf[comp, :, pl.ds(8, 8)] = jnp.zeros((XP, 8, NZ), jnp.float32)
 
-    def true_step(step, slot, wait):
+    def true_step(step, slot, wait, early=lambda: None):
         some_e = functools.partial(update_e, et, ht, kk, jj, amps[step])
         ring_e(slot - 1)
         update_h(et, ht, PX, NX, PY, NY)
         some_e(PX + 1, NX - 1, PY + 8, NY - 8)
+        early()
         wait()
         ring_h(slot)
         some_e(PX, 1, PY, NY)
         some_e(PX + 1, NX - 1, PY, 8)
+
+    def stores():
+        pairs = [(a.at[(comp, *box)], o.at[comp]) for a, o in ((et, e_out), (ht, m_out)) for comp in range(3)]
+        return [pltpu.make_async_copy(src, dst, local.at[1 + i]) for i, (src, dst) in enumerate(pairs)]
 
     load(0).wait()
     lax.fori_loop(0, NX // 2, look_own, 0)
@@ -405,15 +414,15 @@
     pack_h(1)
     peers = sum(there(d).astype(jnp.int32) for d in range(8))
     pl.semaphore_wait(barrier, peers)
-    start(0, 0, parts_e)
-    start(1, 1, parts_h)
+    start(0, 0, 0, parts_e)
+    start(0, 1, 1, parts_h)
     for d in range(8):
         @pl.when(there(d))
         def _(d=d):
             id_copy(d).start()
     clean()
-    arrive(0, 0, False)
-    true_step(0, 1, functools.partial(arrive, 1, 1, True))
+    arrive(0, 0, 0, False)
+    true_step(0, 1, functools.partial(arrive, 0, 1, 1, True))
     def look_around():
         for d in range(8):
             @pl.when(there(OPPOSITE[d]))
@@ -423,16 +432,17 @@
         lax.fori_loop(0, IDS, look_planes, 0)
 
     def block(b, c):
-        size, begin, base = 4 + b, 5 * b - 4, 6 * b - 4
+        first = lax.div(1, b)
+        size, begin, base = 4 - first, 4 * b - 4 + first, 5 * b - 4 + first
         pack_first(base)
-        start(base, 0, parts_e)
+        start(b, base, 0, parts_e)
         lax.fori_loop(0, NX // 4, copy_in, 0)
 
         def free(t, c):
             frame(functools.partial(update_h, ef, hf))
             edges_h()
             pack_h(base + t)
-            one_of(range(1, BLOCK), start, base + t, t, parts_h)
+            one_of(range(1, BLOCK), start, b, base + t, t, parts_h)
 
             @pl.when((b == 1) & (t == 1))
             def _():
@@ -440,40 +450,42 @@
 
             frame(functools.partial(update_e, ef, hf, kk, jj, amps[begin + t - 1]))
             pack_e(base + t)
-            one_of(range(1, BLOCK), start, base + t, t, parts_e)
+            one_of(range(1, BLOCK), start, b, base + t, t, parts_e)
             return c
 
         lax.fori_loop(1, size, free, 0)
         lines_h(functools.partial(update_h, ef, hf))
         edges_h()
         pack_h(base + size)
-        one_of((BLOCK - 1, BLOCK), start, base + size, size, parts_h)
+        one_of((BLOCK - 1, BLOCK), start, b, base + size, size, parts_h)
         clean()
-        arrive(base, 0, False)
+        arrive(b, base, 0, False)
 
         def true(t, c):
             def wait():
                 @pl.when(t < size)
                 def _():
-                    one_of(range(1, BLOCK), arrive, base + t, t, False)
+                    one_of(range(1, BLOCK), arrive, b, base + t, t, False)
 
                 @pl.when(t == size)
                 def _():
-                    one_of((BLOCK - 1, BLOCK), arrive, base + t, t, True)
-
-            true_step(begin + t - 1, base + t, wait)
+                    one_of((BLOCK - 1, BLOCK), arrive, b, base + t, t, True)
+
+            def early():
+                @pl.when(begin + t == STEPS)
+                def _():
+                    for copy in stores()[3:]:
+                        copy.start()
+
+            true_step(begin + t - 1, base + t, wait, early)
             return c
 
         lax.fori_loop(1, size + 1, true, 0)
         return c
 
-    lax.fori_loop(1, 3, block, 0)
-
-    def stores():
-        pairs = [(a.at[(comp, *box)], o.at[comp]) for a, o in ((et, e_out), (ht, m_out)) for comp in range(3)]
-        return [pltpu.make_async_copy(src, dst, local.at[1 + i]) for i, (src, dst) in enumerate(pairs)]
-
-    for copy in stores():
+    lax.fori_loop(1, 4, block, 0)
+
+    for copy in stores()[:3]:
         copy.start()
 
     for d in range(8):
@@ -525,7 +537,7 @@
             *messages,
             *messages,
             pltpu.SemaphoreType.DMA((8,)),
-            pltpu.SemaphoreType.DMA((8, SLOTS)),
+            pltpu.SemaphoreType.DMA((8, TURNS)),
             pltpu.SemaphoreType.DMA((8,)),
             pltpu.SemaphoreType.DMA((8,)),
             pltpu.SemaphoreType.DMA((7,)),

time: 50.7 us -> 49.1 us (0.968)
  Pallas kernels: 49.4 us -> 48.3 us
    pallas_call x1, Pallas kernels: 47.2 us -> 46.1 us  [shards(): pl.pallas_call(kernel, out_shape=(field, field), in_specs=[hbm, hbm, hbm,...]
where the time goes in v4:
time: 49.1 us; the launch traced here: 48.9 us
  Pallas kernels  48.3 us (98%)
  between operations  0.64 us (1%)
    pallas_call x1, Pallas kernels, shards(): pl.pallas_call(kernel, out_shape=(field, field), in_specs=[hbm, hbm, hbm,...  46.1 us
    pallas_call x1, Pallas kernels, shards(): pl.pallas_call(hand_over, out_shape=(field, field), in_specs=[hbm, hbm],...  2.19 us

profile of v4, /device:TPU:57, one launch (start us, length us, event | category | flops | bytes accessed | tf_op | source)
XLA Modules:
  0.0 48.9 jit_solution(1528135980262550778)
XLA Ops:
  0.6 46.1 %shard_map.59 = (f32[3,16,32,128]{3,2,1,0:T(8,128)}, f32[3,16,32,128]{3,2,1,0:T(8,128)}) custom-call(f32[3,16,32,128]{3,2,1,0:T(8,128)} %e_in.1, f32[3,16,32,128]{3,2,1,0:T(8,128)} %m_in.1, s32[16,32,128]{2,1,0:T(8,128)} %ids_in.1, f32[8,9]{1,0:T(8,128)} %table.1), custom_call_target="tpu_custom_call" | custom-call | tf_op jit(solution)/shard_map/pallas_call | solution.py:519
  46.7 2.2 %shard_map.60 = (f32[3,16,32,128]{3,2,1,0:T(8,128)}, f32[3,16,32,128]{3,2,1,0:T(8,128)}) custom-call(f32[3,16,32,128]{3,2,1,0:T(8,128)} %get-tuple-element.4.e_in, f32[3,16,32,128]{3,2,1,0:T(8,128)} %get-tuple-element.5.m_in), custom_call_target="tpu_custom_call" | custom-call | tf_op jit(solution)/shard_map/pallas_call | solution.py:549

commit v5 on v4

--- a/solution.py
+++ b/solution.py
@@ -179,7 +179,7 @@
         return lax.rem(block, 2) * (BLOCK + 1) + depth
 
     def start(block, slot, depth, some):
-        for d in range(8):
+        for d in (N, S, W, E, NW, NE, SW, SE):
             if some(d, depth):
                 @pl.when(there(d))
                 def _(d=d):

time: 49.1 us -> 47.9 us (0.976)
  Pallas kernels: 48.3 us -> 47.1 us
    pallas_call x1, Pallas kernels: 46.1 us -> 44.9 us  [shards(): pl.pallas_call(kernel, out_shape=(field, field), in_specs=[hbm, hbm, hbm,...]
where the time goes in v5:
time: 47.9 us; the launch traced here: 47.7 us
  Pallas kernels  47.1 us (98%)
  between operations  0.64 us (1%)
    pallas_call x1, Pallas kernels, shards(): pl.pallas_call(kernel, out_shape=(field, field), in_specs=[hbm, hbm, hbm,...  44.9 us
    pallas_call x1, Pallas kernels, shards(): pl.pallas_call(hand_over, out_shape=(field, field), in_specs=[hbm, hbm],...  2.19 us

profile of v5, /device:TPU:57, one launch (start us, length us, event | category | flops | bytes accessed | tf_op | source)
XLA Modules:
  0.0 47.7 jit_solution(10307787517593357325)
XLA Ops:
  0.6 44.9 %shard_map.59 = (f32[3,16,32,128]{3,2,1,0:T(8,128)}, f32[3,16,32,128]{3,2,1,0:T(8,128)}) custom-call(f32[3,16,32,128]{3,2,1,0:T(8,128)} %e_in.1, f32[3,16,32,128]{3,2,1,0:T(8,128)} %m_in.1, s32[16,32,128]{2,1,0:T(8,128)} %ids_in.1, f32[8,9]{1,0:T(8,128)} %table.1), custom_call_target="tpu_custom_call" | custom-call | tf_op jit(solution)/shard_map/pallas_call | solution.py:519
  45.6 2.2 %shard_map.60 = (f32[3,16,32,128]{3,2,1,0:T(8,128)}, f32[3,16,32,128]{3,2,1,0:T(8,128)}) custom-call(f32[3,16,32,128]{3,2,1,0:T(8,128)} %get-tuple-element.4.e_in, f32[3,16,32,128]{3,2,1,0:T(8,128)} %get-tuple-element.5.m_in), custom_call_target="tpu_custom_call" | custom-call | tf_op jit(solution)/shard_map/pallas_call | solution.py:549

commit v6 on v5

--- a/solution.py
+++ b/solution.py
@@ -66,7 +66,7 @@
 
 def kernel(e_in, m_in, ids_in, table, e_out, m_out, et, ht, ef, hf, kk, jj, ids, own_x, own_y, ring, total, amps, *rest):
     out, inn = rest[:8], rest[8:16]
-    out_sem, in_sem, id_out, id_in, local = rest[16:]
+    out_sem, in_sem, id_in, local = rest[16:]
     gx, gy = lax.axis_index("gx"), lax.axis_index("gy")
     last_x, last_y = lax.axis_size("gx") - 1, lax.axis_size("gy") - 1
 
@@ -119,7 +119,7 @@
         return pltpu.make_async_remote_copy(
             src_ref=ids_in.at[xs, ys],
             dst_ref=ids.at[xd, yd],
-            send_sem=id_out.at[d],
+            send_sem=out_sem.at[d],
             recv_sem=id_in.at[d],
             device_id=device(d),
             device_id_type=MESH,
@@ -208,7 +208,7 @@
         for d in range(8):
             @pl.when(there(d))
             def _(d=d):
-                rows = 0
+                rows = (IDS if DIRS[d][0] else NX) * (IDS if DIRS[d][1] else NY)
                 for size in SIZES:
                     rows += sum(rows_of(d, m, m == size) for m in range(size + 1))
                 all_of(rows, out_sem.at[d]).wait()
@@ -416,7 +416,7 @@
     pl.semaphore_wait(barrier, peers)
     start(0, 0, 0, parts_e)
     start(0, 1, 1, parts_h)
-    for d in range(8):
+    for d in (N, S, W, E, NW, NE, SW, SE):
         @pl.when(there(d))
         def _(d=d):
             id_copy(d).start()
@@ -488,10 +488,6 @@
     for copy in stores()[:3]:
         copy.start()
 
-    for d in range(8):
-        @pl.when(there(d))
-        def _(d=d):
-            id_copy(d).wait_send()
 
     leave()
     for copy in stores():
@@ -539,7 +535,6 @@
             pltpu.SemaphoreType.DMA((8,)),
             pltpu.SemaphoreType.DMA((8, TURNS)),
             pltpu.SemaphoreType.DMA((8,)),
-            pltpu.SemaphoreType.DMA((8,)),
             pltpu.SemaphoreType.DMA((7,)),
         ],
         compiler_params=pltpu.CompilerParams(

time: 47.9 us -> 47.7 us (level)
  no operation moved by 1% of the time
where the time goes in v6:
time: 47.7 us; the launch traced here: 47.5 us
  Pallas kernels  46.8 us (98%)
  between operations  0.64 us (1%)
    pallas_call x1, Pallas kernels, shards(): pl.pallas_call(kernel, out_shape=(field, field), in_specs=[hbm, hbm, hbm,...  44.6 us
    pallas_call x1, Pallas kernels, shards(): pl.pallas_call(hand_over, out_shape=(field, field), in_specs=[hbm, hbm],...  2.19 us

profile of v6, /device:TPU:57, one launch (start us, length us, event | category | flops | bytes accessed | tf_op | source)
XLA Modules:
  0.0 47.5 jit_solution(45250952580698239)
XLA Ops:
  0.6 44.6 %shard_map.59 = (f32[3,16,32,128]{3,2,1,0:T(8,128)}, f32[3,16,32,128]{3,2,1,0:T(8,128)}) custom-call(f32[3,16,32,128]{3,2,1,0:T(8,128)} %e_in.1, f32[3,16,32,128]{3,2,1,0:T(8,128)} %m_in.1, s32[16,32,128]{2,1,0:T(8,128)} %ids_in.1, f32[8,9]{1,0:T(8,128)} %table.1), custom_call_target="tpu_custom_call" | custom-call | tf_op jit(solution)/shard_map/pallas_call | solution.py:515
  45.3 2.2 %shard_map.60 = (f32[3,16,32,128]{3,2,1,0:T(8,128)}, f32[3,16,32,128]{3,2,1,0:T(8,128)}) custom-call(f32[3,16,32,128]{3,2,1,0:T(8,128)} %get-tuple-element.4.e_in, f32[3,16,32,128]{3,2,1,0:T(8,128)} %get-tuple-element.5.m_in), custom_call_target="tpu_custom_call" | custom-call | tf_op jit(solution)/shard_map/pallas_call | solution.py:544
